TPU v7x, 512 devices: a whole 4x8x8 slice. The times are simulated.
512 devices in a mesh: blk: 32 (over y, x), col: 16 (over z, core).
Axes of the slice: x: 4, y: 8, z: 8, core: 2. Of those that a mesh axis runs over, the one named last changes fastest.
Arguments:
- visit_cov: bfloat16 [32768, 128], P('blk'), may hold values from -6 to 6
- tumor_size: bfloat16 [32768], P('blk'), may hold values from -6 to 6
- visit_weight: bfloat16 [32768], P('blk'), may hold values from 0.5 to 2
- visit_owner: int32 [32768, 1], P('blk'), may hold values from 0 to 31; in each aligned block of 1024 rows (0 to 1023, 1024 to 2047, ...) at most 64 rows name the same one
- visit_patient: int32 [32768], P('blk'), may hold values from 0 to 127
- inducing_freq: bfloat16 [128, 2048], P(None, 'col'), may hold values from -1.5 to 1.5
- inducing_phase: bfloat16 [2048], P('col'), may hold values from -3.140625 to 3.140625
- node_cov: bfloat16 [4096, 16, 128], P('blk'), may hold values from -6 to 6
- event_time: float32 [4096], P('blk'), may hold values from 0.2 to 2
- event_flag: int32 [4096], P('blk'), may hold values 0 or 1
Outputs:
- loglik: float32 [4096], P('blk')
- mean_weights: float32 [2048], P('col')
Inputs may be any that keep to these rules, and one draw needn't show every extreme that they name: `visit_owner`: among the visits entering one index of blk, no owner is named more than 64 times, a bound that some block reaches.
All inputs are finite; a program needn't handle non-finite values. No bound on the sum of `event_flag` on one device may be relied on, other than what follows from the above.
Results may differ from a plain program's by a relative error of at most 0.003.
Values may be sent and summed in bfloat16 or wider, within the bound.
No kernel may reach another device: no remote copies, remote signals or barrier semaphores. Data moves between devices by JAX's collectives and lax.ppermute only.
A program may use at most 64 MiB of HBM per device.

v0:
```python
import math
import jax
import jax.numpy as jnp
from jax import lax
from jax.sharding import PartitionSpec as P

ITERS = 3
SQRT_TWO = math.sqrt(2.0)
LOG_SHAPE = math.log(1.5)
LINK = 0.4


def features(covariates, frequency, phases):
    angles = jnp.dot(covariates, frequency, preferred_element_type=jnp.float32) + phases.astype(
        jnp.float32
    )
    return (SQRT_TWO * jnp.cos(angles)).astype(jnp.bfloat16)


def norm_of(vector):
    return lax.psum(jnp.sum(vector * vector), "col")


def on_device(
    visit_cov,
    tumor_size,
    visit_weight,
    visit_owner,
    visit_patient,
    inducing_freq,
    inducing_phase,
    node_cov,
    event_time,
    event_flag,
):
    blocks = lax.axis_size("blk")
    visits_here = visit_cov.shape[0]
    width_in = visit_cov.shape[1]
    total_visits = visits_here * blocks
    owners = visit_owner[:, 0]
    owner_table = (owners[:, None] == jnp.arange(blocks, dtype=jnp.int32)[None, :]).astype(
        jnp.int32
    )
    capacity = 2 * visits_here // blocks
    slots = blocks * capacity
    ranking = jnp.cumsum(owner_table, axis=0) - 1
    target = owners * capacity + jnp.sum(owner_table * ranking, axis=1)
    cov_buffer = (
        jnp.zeros((slots, width_in), jnp.bfloat16)
        .at[target]
        .set(visit_cov)
        .reshape(blocks, capacity, width_in)
    )
    packed = jnp.stack([visit_weight, tumor_size, visit_patient.astype(jnp.bfloat16)], axis=1)
    val_buffer = (
        jnp.zeros((slots, 3), jnp.bfloat16)
        .at[target]
        .set(packed)
        .reshape(blocks, capacity, 3)
        .transpose(0, 2, 1)
    )
    cov_in, val_in = (
        lax.all_to_all(cov_buffer, "blk", split_axis=0, concat_axis=0, tiled=True),
        lax.all_to_all(val_buffer, "blk", split_axis=0, concat_axis=0, tiled=True),
    )
    cov_in = cov_in.reshape(slots, width_in)
    weight_in = val_in[:, 0, :].reshape(slots).astype(jnp.float32)
    size_in = val_in[:, 1, :].reshape(slots).astype(jnp.float32)
    patient_in = val_in[:, 2, :].reshape(slots).astype(jnp.int32)
    row_count = cov_in.shape[0]
    phi_local = features(cov_in, inducing_freq, inducing_phase)
    phi_wide = phi_local.astype(jnp.float32)
    rhs_local = jnp.dot(weight_in * size_in, phi_wide, precision=lax.Precision.HIGHEST)
    local_cols = inducing_freq.shape[1]
    inducing = local_cols * lax.axis_size("col")
    freq_all, phase_all = (
        lax.all_gather(inducing_freq, "col", axis=1, tiled=True),
        lax.all_gather(inducing_phase, "col", axis=0, tiled=True),
    )
    step_rows = min(512, row_count)

    def add_block(index, gram):
        first = index * step_rows
        rows_cov = lax.dynamic_slice_in_dim(cov_in, first, step_rows, 0)
        rows_weight = lax.dynamic_slice_in_dim(weight_in, first, step_rows, 0)
        rows_phi = lax.dynamic_slice_in_dim(phi_local, first, step_rows, 0)
        full_phi = features(rows_cov, freq_all, phase_all)
        weighted = (rows_weight[:, None] * full_phi.astype(jnp.float32)).astype(jnp.bfloat16)
        return gram + lax.dot_general(
            weighted, rows_phi, (((0,), (0,)), ((), ())), preferred_element_type=jnp.float32
        )

    gram = lax.fori_loop(
        0, row_count // step_rows, add_block, jnp.zeros((inducing, local_cols), jnp.float32)
    )
    gram, rhs = lax.psum((gram, rhs_local), "blk")
    gram = gram / total_visits
    rhs = rhs / math.sqrt(total_visits)
    solution = jnp.zeros((local_cols,), jnp.float32)
    residual = rhs
    direction = rhs
    norm_now = norm_of(residual)
    for turn in range(ITERS):
        whole = lax.all_gather(direction, "col", axis=0, tiled=True)
        image = direction + jnp.dot(whole, gram, precision=lax.Precision.HIGHEST)
        alpha = norm_now / lax.psum(jnp.sum(direction * image), "col")
        solution = solution + alpha * direction
        residual = residual - alpha * image
        norm_next = norm_of(residual)
        direction = residual + norm_next / norm_now * direction
        norm_now = norm_next
    nodes_flat = node_cov.reshape(-1, width_in)
    node_phi = features(nodes_flat, inducing_freq, inducing_phase)
    fit_part = jnp.dot(phi_wide, solution, precision=lax.Precision.HIGHEST)
    node_part = jnp.dot(node_phi.astype(jnp.float32), solution, precision=lax.Precision.HIGHEST)
    fitted, node_value = lax.psum((fit_part, node_part), "col")
    fitted = fitted / math.sqrt(inducing)
    node_value = node_value / math.sqrt(inducing)
    patients_here = event_time.shape[0]
    nodes_count = node_cov.shape[1]
    patient_table = (
        patient_in[:, None] == jnp.arange(patients_here, dtype=jnp.int32)[None, :]
    ).astype(jnp.float32)
    residual_term = weight_in * (size_in - fitted)
    numer = jnp.dot(residual_term, patient_table, precision=lax.Precision.HIGHEST)
    denom = 1.0 + jnp.dot(weight_in, patient_table, precision=lax.Precision.HIGHEST)
    effect = numer / denom
    grid = (
        event_time[:, None]
        * (jnp.arange(nodes_count).astype(jnp.float32)[None, :] + 1.0)
        / nodes_count
    )
    eta = (
        LOG_SHAPE
        + 0.5 * jnp.log(grid)
        + LINK * (node_value.reshape(patients_here, nodes_count) + effect[:, None])
    )
    loglik = event_flag.astype(jnp.float32) * eta[:, -1] - event_time / nodes_count * jnp.sum(
        jnp.exp(eta), axis=1
    )
    return (loglik, solution)


def solution(mesh):
    in_specs = (
        P("blk", None),
        P("blk"),
        P("blk"),
        P("blk", None),
        P("blk"),
        P(None, "col"),
        P("col"),
        P("blk", None, None),
        P("blk"),
        P("blk"),
    )
    out_specs = (P("blk"), P("col"))
    return jax.shard_map(
        on_device, mesh=mesh, in_specs=in_specs, out_specs=out_specs, check_vma=False
    )
```

profile of v0, /device:TPU:16, one launch (start us, length us, event | category | flops | bytes accessed | tf_op | source)
XLA Modules:
  0.0 532.7 jit_solution(2748140927083613573)
XLA Ops:
  8.0 9.0 %reduce-window.6 = s32[32,8,128]{2,1,0:T(8,128)S(1)} reduce-window(s32[32,8,128]{2,1,0:T(8,128)S(1)} %fusion.35, s32[]{:T(128)} %constant.72.clone.1), window={size=1x1x128 pad=0_0x0_0x127_0}, to_apply=%region_0.0 | reduce-window | flops 4161536 | bytes 262148 | tf_op jit(solution)/shard_map/reduce-window
  22.1 10.1 %all-to-all-start = ((bf16[32,3,64]{2,1,0:T(4,128)(2,1)}), bf16[32,3,64]{2,1,0:T(4,128)(2,1)S(1)}, u32[]{:S(2)}, u32[]{:S(2)}) async-start(bf16[32,3,64]{2,1,0:T(4,128)(2,1)} %bitcast.8), calls=%async_computation | async-start | bytes 65536 | tf_op jit(solution)/shard_map/all_to_all | solution.py:64
  32.1 4.3 scatter_custom_fusion.1
  40.0 6.2 %all-to-all-start.1 = ((bf16[32,64,128]{2,1,0:T(8,128)(2,1)}), bf16[32,64,128]{2,1,0:T(8,128)(2,1)S(1)}, u32[]{:S(2)}, u32[]{:S(2)}) async-start(bf16[32,64,128]{2,1,0:T(8,128)(2,1)} %bitcast.10), calls=%async_computation.1 | async-start | bytes 1048576 | tf_op jit(solution)/shard_map/all_to_all | solution.py:63
  46.3 23.1 %all-gather.1 = bf16[16,1,128]{2,1,0:T(2,128)(2,1)S(1)} all-gather(bf16[1,1,128]{2,1,0:T(2,128)(2,1)S(1)} %bitcast.121), channel_id=1, replica_groups=mesh['blk'=32,'col'=16] {'col'}, dimensions={0}, use_global_device_ids=true | all-gather | bytes 4352 | tf_op jit(solution)/shard_map/all_gather | solution.py:78
  69.4 15.9 %all_gather.16 = bf16[128,2048]{1,0:T(8,128)(2,1)S(1)} all-gather(bf16[128,128]{1,0:T(8,128)(2,1)S(1)} %copy-done.4), channel_id=1, replica_groups=mesh['blk'=32,'col'=16] {'col'}, dimensions={1}, use_global_device_ids=true | all-gather | bytes 557056 | tf_op jit(solution)/shard_map/all_gather | solution.py:77
  85.5 3.9 fusion.11
  89.3 61.9 %while.14 = (s32[]{:T(128)}, f32[2048,128]{1,0:T(8,128)S(1)}, f32[2048]{0:T(1024)S(1)}, bf16[2048,128]{1,0:T(8,128)(2,1)S(1)}, bf16[128,2048]{1,0:T(8,128)(2,1)S...) while((s32[]{:T(128)}, f32[2048,128]{1,0:T(8,128)S(1)}, ...), condition=%wide.region_9.10_spmd.clone, body=%wide.region_8.9_spmd.clone.sunk | while | flops 543688704 | bytes 2911912 | solution.py:93
  89.6 15.2 %convolution_add_fusion.4 = f32[2048,128]{1,0:T(8,128)S(1)} fusion(bf16[128,2048]{1,0:T(8,128)(2,1)S(1)} %get-tuple-element.249, f32[2048]{0:T(1024)S(1)} %convert_element_type.131, f32[512]{0:T(512)S(1)} %dynamic_slice.34, f32[2048,128]{1,0:T(8,128)S(1)} %get-tuple-element.235, pred[]{:T(512)S(6)} %compare.3, ...), kind=kOutput, calls=%fused_computation.4.clone.1 | convolution fusion | flops 543686656 | bytes 2895360 | tf_op jit(solution)/shard_map/while/body/eval_jaxpr/dot_general | solution.py:89
  105.0 15.3 %convolution_add_fusion.4 = f32[2048,128]{1,0:T(8,128)S(1)} fusion(bf16[128,2048]{1,0:T(8,128)(2,1)S(1)} %get-tuple-element.249, f32[2048]{0:T(1024)S(1)} %convert_element_type.131, f32[512]{0:T(512)S(1)} %dynamic_slice.34, f32[2048,128]{1,0:T(8,128)S(1)} %get-tuple-element.235, pred[]{:T(512)S(6)} %compare.3, ...), kind=kOutput, calls=%fused_computation.4.clone.1 | convolution fusion | flops 543686656 | bytes 2895360 | tf_op jit(solution)/shard_map/while/body/eval_jaxpr/dot_general | solution.py:89
  120.3 15.3 %convolution_add_fusion.4 = f32[2048,128]{1,0:T(8,128)S(1)} fusion(bf16[128,2048]{1,0:T(8,128)(2,1)S(1)} %get-tuple-element.249, f32[2048]{0:T(1024)S(1)} %convert_element_type.131, f32[512]{0:T(512)S(1)} %dynamic_slice.34, f32[2048,128]{1,0:T(8,128)S(1)} %get-tuple-element.235, pred[]{:T(512)S(6)} %compare.3, ...), kind=kOutput, calls=%fused_computation.4.clone.1 | convolution fusion | flops 543686656 | bytes 2895360 | tf_op jit(solution)/shard_map/while/body/eval_jaxpr/dot_general | solution.py:89
  135.7 15.3 %convolution_add_fusion.4 = f32[2048,128]{1,0:T(8,128)S(1)} fusion(bf16[128,2048]{1,0:T(8,128)(2,1)S(1)} %get-tuple-element.249, f32[2048]{0:T(1024)S(1)} %convert_element_type.131, f32[512]{0:T(512)S(1)} %dynamic_slice.34, f32[2048,128]{1,0:T(8,128)S(1)} %get-tuple-element.235, pred[]{:T(512)S(6)} %compare.3, ...), kind=kOutput, calls=%fused_computation.4.clone.1 | convolution fusion | flops 543686656 | bytes 2895360 | tf_op jit(solution)/shard_map/while/body/eval_jaxpr/dot_general | solution.py:89
  152.3 3.9 fusion.10
  156.8 62.8 %psum.70 = f32[128]{0:T(128)S(1)} all-reduce(f32[128]{0:T(128)S(1)} %convolution_bitcast_fusion.5), channel_id=1, replica_groups=mesh['blk'=32,'col'=16] {'blk'}, use_global_device_ids=true, to_apply=%region_5.6 | all-reduce | flops 128 | bytes 1024 | tf_op jit(solution)/shard_map/psum | solution.py:96
  219.6 15.7 %all-gather = f32[16,1,128]{2,1,0:T(1,128)S(1)} all-gather(f32[1,1,128]{2,1,0:T(1,128)S(1)} %fusion.50), channel_id=1, replica_groups=mesh['blk'=32,'col'=16] {'col'}, dimensions={0}, use_global_device_ids=true | all-gather | bytes 8704 | tf_op jit(solution)/shard_map/all_gather | solution.py:104
  235.3 73.6 %all-reduce.4.cloned.1.call-done = f32[2048,128]{1,0:T(8,128)} async-done(((f32[2048,128]{1,0:T(8,128)}), f32[2048,128]{1,0:T(8,128)}) %all-reduce.4.cloned.1.call-update) | async-done | bytes 1048592 | tf_op jit(solution)/shard_map/psum | solution.py:96
  311.5 24.8 %all-reduce.1 = (f32[]{:T(128)}, f32[]{:T(128)}) all-reduce(f32[]{:T(128)} %get-tuple-element.152, f32[]{:T(128)} %get-tuple-element.151), channel_id=1, replica_groups=mesh['blk'=32,'col'=16] {'col'}, use_global_device_ids=true, to_apply=%region_7.8 | all-reduce | flops 2 | bytes 16 | tf_op jit(solution)/shard_map/psum | solution.py:21
  338.2 24.5 %psum.74 = f32[]{:T(128)} all-reduce(f32[]{:T(128)} %get-tuple-element.173), channel_id=1, replica_groups=mesh['blk'=32,'col'=16] {'col'}, use_global_device_ids=true, to_apply=%region_14.15 | all-reduce | flops 1 | bytes 8 | tf_op jit(solution)/shard_map/psum | solution.py:21
  364.1 14.4 %all-gather.2 = f32[16,1,128]{2,1,0:T(1,128)S(1)} all-gather(f32[1,1,128]{2,1,0:T(1,128)S(1)} %bitcast.116), channel_id=1, replica_groups=mesh['blk'=32,'col'=16] {'col'}, dimensions={0}, use_global_device_ids=true | all-gather | bytes 8704 | tf_op jit(solution)/shard_map/all_gather | solution.py:104
  379.7 27.3 %psum.75 = f32[]{:T(128)} all-reduce(f32[]{:T(128)} %get-tuple-element.176), channel_id=1, replica_groups=mesh['blk'=32,'col'=16] {'col'}, use_global_device_ids=true, to_apply=%region_16.17 | all-reduce | flops 1 | bytes 8 | tf_op jit(solution)/shard_map/psum | solution.py:106
  409.0 24.2 %psum.76 = f32[]{:T(128)} all-reduce(f32[]{:T(128)} %multiply_reduce_fusion), channel_id=1, replica_groups=mesh['blk'=32,'col'=16] {'col'}, use_global_device_ids=true, to_apply=%region_18.19 | all-reduce | flops 1 | bytes 8 | tf_op jit(solution)/shard_map/psum | solution.py:21
  434.5 14.1 %all-gather.3 = f32[16,1,128]{2,1,0:T(1,128)S(1)} all-gather(f32[1,1,128]{2,1,0:T(1,128)S(1)} %bitcast.117), channel_id=1, replica_groups=mesh['blk'=32,'col'=16] {'col'}, dimensions={0}, use_global_device_ids=true | all-gather | bytes 8704 | tf_op jit(solution)/shard_map/all_gather | solution.py:104
  449.8 26.1 %psum.77 = f32[]{:T(128)} all-reduce(f32[]{:T(128)} %fusion.21), channel_id=1, replica_groups=mesh['blk'=32,'col'=16] {'col'}, use_global_device_ids=true, to_apply=%region_20.21 | all-reduce | flops 1 | bytes 8 | tf_op jit(solution)/shard_map/psum | solution.py:106
  478.3 45.7 %all-reduce = (f32[2048]{0:T(1024)S(1)}, f32[2048]{0:T(1024)S(1)}) all-reduce(f32[2048]{0:T(1024)S(1)} %bitcast.112, f32[2048]{0:T(1024)S(1)} %bitcast.111), channel_id=1, replica_groups=mesh['blk'=32,'col'=16] {'col'}, use_global_device_ids=true, to_apply=%region_21.22 | all-reduce | flops 4096 | bytes 32768 | tf_op jit(solution)/shard_map/psum | solution.py:116
  (85 shorter events, 20.7 us)
Async XLA Ops:
  7.2 145.1 %copy-start = (bf16[128,16,128]{2,1,0:T(8,128)(2,1)S(1)}, bf16[128,16,128]{2,1,0:T(8,128)(2,1)}, u32[]{:S(2)}) copy-start(bf16[128,16,128]{2,1,0:T(8,128)(2,1)} %param.19) | copy-start | bytes 1572868
  7.2 10.3 %copy-start.3 = (s32[1024,1]{0,1:T(1,128)S(1)}, s32[1024,1]{0,1:T(1,128)}, u32[]{:S(2)}) copy-start(s32[1024,1]{0,1:T(1,128)} %param.15) | copy-start | bytes 12292
  7.2 10.3 %copy-start.6 = (s32[1024]{0:T(1024)S(1)}, s32[1024]{0:T(1024)}, u32[]{:S(2)}) copy-start(s32[1024]{0:T(1024)} %param.16) | copy-start | bytes 12292
  7.2 10.4 %copy-start.7 = (bf16[1024]{0:T(1024)(128)(2,1)S(1)}, bf16[1024]{0:T(1024)(128)(2,1)}, u32[]{:S(2)}) copy-start(bf16[1024]{0:T(1024)(128)(2,1)} %param.14) | copy-start | bytes 6148
  7.2 10.4 %copy-start.8 = (bf16[1024]{0:T(1024)(128)(2,1)S(1)}, bf16[1024]{0:T(1024)(128)(2,1)}, u32[]{:S(2)}) copy-start(bf16[1024]{0:T(1024)(128)(2,1)} %param.13) | copy-start | bytes 6148
  21.2 25.1 %copy-start.10 = (bf16[128]{0:T(256)(128)(2,1)S(1)}, bf16[128]{0:T(256)(128)(2,1)}, u32[]{:S(2)}) copy-start(bf16[128]{0:T(256)(128)(2,1)} %param.18) | copy-start | bytes 772
  21.2 48.2 %copy-start.4 = (bf16[128,128]{1,0:T(8,128)(2,1)S(1)}, bf16[128,128]{1,0:T(8,128)(2,1)}, u32[]{:S(2)}) copy-start(bf16[128,128]{1,0:T(8,128)(2,1)} %param.17) | copy-start | bytes 98308
  22.1 17.9 %all-to-all-start = ((bf16[32,3,64]{2,1,0:T(4,128)(2,1)}), bf16[32,3,64]{2,1,0:T(4,128)(2,1)S(1)}, u32[]{:S(2)}, u32[]{:S(2)}) async-start(bf16[32,3,64]{2,1,0:T(4,128)(2,1)} %bitcast.8), calls=%async_computation | async-start | bytes 65536 | tf_op jit(solution)/shard_map/all_to_all | solution.py:64
  40.0 45.5 %all-to-all-start.1 = ((bf16[32,64,128]{2,1,0:T(8,128)(2,1)}), bf16[32,64,128]{2,1,0:T(8,128)(2,1)S(1)}, u32[]{:S(2)}, u32[]{:S(2)}) async-start(bf16[32,64,128]{2,1,0:T(8,128)(2,1)} %bitcast.10), calls=%async_computation.1 | async-start | bytes 1048576 | tf_op jit(solution)/shard_map/all_to_all | solution.py:63
  46.3 262.7 %all-reduce.4.cloned.1.call-start = ((), (), s32[]{:S(2)}) async-start(), calls=%async_computation.2 | async-start | bytes 2097152 | tf_op jit(solution)/shard_map/psum | solution.py:96
  151.2 1.0 copy-start.2
  308.9 69.6 %copy-start.1 = (f32[2048,128]{1,0:T(8,128)S(1)}, f32[2048,128]{1,0:T(8,128)}, u32[]{:S(2)}) copy-start(f32[2048,128]{1,0:T(8,128)} %all-reduce.4.cloned.1.call-done) | copy-start | bytes 3145732
  449.8 75.4 %copy-start.9 = (f32[128]{0:T(128)S(1)}, f32[128]{0:T(128)}, u32[]{:S(2)}) copy-start(f32[128]{0:T(128)} %param.20) | copy-start | bytes 1540
  449.8 75.5 %copy-start.11 = (s32[128]{0:T(128)S(1)}, s32[128]{0:T(128)}, u32[]{:S(2)}) copy-start(s32[128]{0:T(128)} %param.21) | copy-start | bytes 1540
  477.2 48.6 %copy-start.5 = (f32[128]{0:T(128)}, f32[128]{0:T(128)S(1)}, u32[]{:S(2)}) copy-start(f32[128]{0:T(128)S(1)} %multiply_add_fusion.1) | copy-start | bytes 1540
Sparse Core Ops, SparseCore 0:
  152.4 156.4 all-reduce.3
where the time goes:
time: 533 us
  blocking collectives  318 us (60%)
  waiting for transfers between devices  77.2 us (14%)
  matrix products  76.3 us (14%)
  between operations  21.1 us (4%)
  starting transfers between devices  16.3 us (3%)
  other arithmetic  12 us (2%)
  local copies, waits for them, and re-layouts  10.9 us (2%)
    psum x1, waiting for transfers between devices, on_device(): gram, rhs = lax.psum((gram, rhs_local), 'blk')  73.6 us
    psum x3, blocking collectives, norm_of(): return lax.psum(jnp.sum(vector * vector), 'col')  73.4 us
    psum x1, blocking collectives, on_device(): gram, rhs = lax.psum((gram, rhs_local), 'blk')  62.8 us
    dot_general x4, matrix products, add_block(): lax.dot_general(weighted, rows_phi, (((0,), (0,)), ((), ())), preferred_e...  61.1 us
    psum x2, blocking collectives, on_device(): alpha = norm_now / lax.psum(jnp.sum(direction * image), 'col')  53.3 us
    psum x1, blocking collectives, on_device(): fitted, node_value = lax.psum((fit_part, node_part), 'col')  45.7 us
    all_gather x3, blocking collectives, on_device(): whole = lax.all_gather(direction, 'col', axis=0, tiled=True)  44.2 us
    all_gather x1, blocking collectives, on_device(): lax.all_gather(inducing_phase, 'col', axis=0, tiled=True)  23.1 us
  transfers between devices with their start and end apart: 3, of which 2 were waited for; matrix products, arithmetic and copies ran while one was open for 2% of the time, Pallas kernels for 0%

commit v1 on v0

--- a/solution.py
+++ b/solution.py
@@ -8,6 +8,22 @@
 SQRT_TWO = math.sqrt(2.0)
 LOG_SHAPE = math.log(1.5)
 LINK = 0.4
+
+
+def gather_around(x, axis, dim):
+    ways, here, lap = (lax.axis_size(axis), lax.axis_index(axis), x.shape[dim])
+    dims = [n * ways if d == dim else n for d, n in enumerate(x.shape)]
+    full = lax.dynamic_update_slice_in_dim(jnp.zeros(dims, x.dtype), x, here * lap, axis=dim)
+    going_up = going_down = x
+    for far in range(1, ways // 2 + 1):
+        going_up = lax.ppermute(going_up, axis, [(d, (d + 1) % ways) for d in range(ways)])
+        full = lax.dynamic_update_slice_in_dim(full, going_up, (here - far) % ways * lap, axis=dim)
+        if 2 * far < ways:
+            going_down = lax.ppermute(going_down, axis, [(d, (d - 1) % ways) for d in range(ways)])
+            full = lax.dynamic_update_slice_in_dim(
+                full, going_down, (here + far) % ways * lap, axis=dim
+            )
+    return full
 
 
 def features(covariates, frequency, phases):
@@ -74,7 +90,7 @@
     local_cols = inducing_freq.shape[1]
     inducing = local_cols * lax.axis_size("col")
     freq_all, phase_all = (
-        lax.all_gather(inducing_freq, "col", axis=1, tiled=True),
+        gather_around(inducing_freq, "col", 1),
         lax.all_gather(inducing_phase, "col", axis=0, tiled=True),
     )
     step_rows = min(512, row_count)

time: 533 us -> 551 us (1.034)
  starting transfers between devices: 16.3 us -> 46.7 us
  blocking collectives: 318 us -> 294 us
  waiting for transfers between devices: 77.2 us -> 88.2 us
    ppermute x0 -> x15, starting transfers between devices: none -> 26.8 us  [the longest x7 26.8 us: gather_around(): lax.ppermute(going_down, axis, [(d, (d - 1) % ways) for d in range(ways)])]
    all_gather x1 -> x0, blocking collectives: 15.9 us -> none  [on_device(): lax.all_gather(inducing_freq, 'col', axis=1, tiled=True)]
    ppermute x0 -> x15, waiting for transfers between devices: none -> 13.3 us  [the longest x8 10.6 us: gather_around(): lax.ppermute(going_up, axis, [(d, (d + 1) % ways) for d in range(ways)])]
    all_gather x1, blocking collectives: 23.1 us -> 16.3 us  [on_device(): lax.all_gather(inducing_phase, 'col', axis=0, tiled=True)]
  transfers between devices with their start and end apart: 3 -> 18, of which waited for: 2 -> 13; matrix products, arithmetic and copies ran while one was open for 2% -> 4% of each run, Pallas kernels for 0% -> 0%
where the time goes in v1:
time: 551 us; the launch traced here: 550 us
  blocking collectives  294 us (53%)
  waiting for transfers between devices  88.2 us (16%)
  matrix products  76.3 us (14%)
  starting transfers between devices  46.7 us (8%)
  between operations  21.4 us (4%)
  other arithmetic  12 us (2%)
  local copies, waits for them, and re-layouts  11.2 us (2%)
    psum x1, waiting for transfers between devices, on_device(): gram, rhs = lax.psum((gram, rhs_local), 'blk')  74.9 us
    psum x3, blocking collectives, norm_of(): return lax.psum(jnp.sum(vector * vector), 'col')  73.4 us
    psum x1, blocking collectives, on_device(): gram, rhs = lax.psum((gram, rhs_local), 'blk')  62.8 us
    dot_general x4, matrix products, add_block(): lax.dot_general(weighted, rows_phi, (((0,), (0,)), ((), ())), preferred_e...  61 us
    psum x2, blocking collectives, on_device(): alpha = norm_now / lax.psum(jnp.sum(direction * image), 'col')  53.3 us
    psum x1, blocking collectives, on_device(): fitted, node_value = lax.psum((fit_part, node_part), 'col')  45.7 us
    all_gather x3, blocking collectives, on_device(): whole = lax.all_gather(direction, 'col', axis=0, tiled=True)  42.5 us
    ppermute x7, starting transfers between devices, gather_around(): lax.ppermute(going_down, axis, [(d, (d - 1) % ways) for d in range(ways)])  26.8 us
  transfers between devices with their start and end apart: 18, of which 13 were waited for; matrix products, arithmetic and copies ran while one was open for 4% of the time, Pallas kernels for 0%

profile of v1, /device:TPU:16, one launch (start us, length us, event | category | flops | bytes accessed | tf_op | source)
XLA Modules:
  0.0 550.4 jit_solution(13952724035080756659)
XLA Ops:
  7.2 8.5 %collective-permute-start.1 = (bf16[128,128]{1,0:T(8,128)(2,1)}, bf16[128,128]{1,0:T(8,128)(2,1)S(1)}, u32[]{:S(2)}, u32[]{:S(2)}) collective-permute-start(bf16[128,128]{1,0:T(8,128)(2,1)} %param.17), channel_id=1, source_target_pairs={{0,15},{1,0},{2,1},{3,2},{4,3},{5,4},{6,5},{7,6},{8,7},{9,8},{10,9... | collective-permute-start | bytes 98312 | tf_op jit(solution)/shard_map/ppermute | solution.py:22
  16.4 9.0 %reduce-window.6 = s32[32,8,128]{2,1,0:T(8,128)S(1)} reduce-window(s32[32,8,128]{2,1,0:T(8,128)S(1)} %fusion.35, s32[]{:T(128)} %constant.160.clone.1), window={size=1x1x128 pad=0_0x0_0x127_0}, to_apply=%region_0.0 | reduce-window | flops 4161536 | bytes 262148 | tf_op jit(solution)/shard_map/reduce-window
  30.5 10.1 %all-to-all-start = ((bf16[32,3,64]{2,1,0:T(4,128)(2,1)}), bf16[32,3,64]{2,1,0:T(4,128)(2,1)S(1)}, u32[]{:S(2)}, u32[]{:S(2)}) async-start(bf16[32,3,64]{2,1,0:T(4,128)(2,1)} %bitcast.8), calls=%async_computation | async-start | bytes 65536 | tf_op jit(solution)/shard_map/all_to_all | solution.py:80
  41.0 4.3 scatter_custom_fusion.1
  45.3 16.3 %all-gather.1 = bf16[16,1,128]{2,1,0:T(2,128)(2,1)S(1)} all-gather(bf16[1,1,128]{2,1,0:T(2,128)(2,1)S(1)} %bitcast.121), channel_id=1, replica_groups=mesh['blk'=32,'col'=16] {'col'}, dimensions={0}, use_global_device_ids=true | all-gather | bytes 4352 | tf_op jit(solution)/shard_map/all_gather | solution.py:94
  61.6 9.8 %all-to-all-start.1 = ((bf16[32,64,128]{2,1,0:T(8,128)(2,1)}), bf16[32,64,128]{2,1,0:T(8,128)(2,1)S(1)}, u32[]{:S(2)}, u32[]{:S(2)}) async-start(bf16[32,64,128]{2,1,0:T(8,128)(2,1)} %bitcast.10), calls=%async_computation.1 | async-start | bytes 1048576 | tf_op jit(solution)/shard_map/all_to_all | solution.py:79
  99.5 3.9 collective-permute-done.14
  103.5 3.9 fusion.11
  107.4 61.9 %while.14 = (s32[]{:T(128)}, f32[2048,128]{1,0:T(8,128)S(1)}, f32[2048]{0:T(1024)S(1)}, bf16[2048,128]{1,0:T(8,128)(2,1)S(1)}, bf16[128,2048]{1,0:T(8,128)(2,1)S...) while((s32[]{:T(128)}, f32[2048,128]{1,0:T(8,128)S(1)}, ...), condition=%wide.region_9.10_spmd.clone, body=%wide.region_8.9_spmd.clone.sunk | while | flops 543688704 | bytes 2911912 | solution.py:109
  107.7 15.2 %convolution_add_fusion.4 = f32[2048,128]{1,0:T(8,128)S(1)} fusion(bf16[128,2048]{1,0:T(8,128)(2,1)S(1)} %get-tuple-element.249, f32[2048]{0:T(1024)S(1)} %convert_element_type.131, f32[512]{0:T(512)S(1)} %dynamic_slice.34, f32[2048,128]{1,0:T(8,128)S(1)} %get-tuple-element.235, pred[]{:T(512)S(6)} %compare.18, ...), kind=kOutput, calls=%fused_computation.4.clone.1 | convolution fusion | flops 543686656 | bytes 2895360 | tf_op jit(solution)/shard_map/while/body/eval_jaxpr/dot_general | solution.py:105
  123.0 15.3 %convolution_add_fusion.4 = f32[2048,128]{1,0:T(8,128)S(1)} fusion(bf16[128,2048]{1,0:T(8,128)(2,1)S(1)} %get-tuple-element.249, f32[2048]{0:T(1024)S(1)} %convert_element_type.131, f32[512]{0:T(512)S(1)} %dynamic_slice.34, f32[2048,128]{1,0:T(8,128)S(1)} %get-tuple-element.235, pred[]{:T(512)S(6)} %compare.18, ...), kind=kOutput, calls=%fused_computation.4.clone.1 | convolution fusion | flops 543686656 | bytes 2895360 | tf_op jit(solution)/shard_map/while/body/eval_jaxpr/dot_general | solution.py:105
  138.4 15.3 %convolution_add_fusion.4 = f32[2048,128]{1,0:T(8,128)S(1)} fusion(bf16[128,2048]{1,0:T(8,128)(2,1)S(1)} %get-tuple-element.249, f32[2048]{0:T(1024)S(1)} %convert_element_type.131, f32[512]{0:T(512)S(1)} %dynamic_slice.34, f32[2048,128]{1,0:T(8,128)S(1)} %get-tuple-element.235, pred[]{:T(512)S(6)} %compare.18, ...), kind=kOutput, calls=%fused_computation.4.clone.1 | convolution fusion | flops 543686656 | bytes 2895360 | tf_op jit(solution)/shard_map/while/body/eval_jaxpr/dot_general | solution.py:105
  153.8 15.3 %convolution_add_fusion.4 = f32[2048,128]{1,0:T(8,128)S(1)} fusion(bf16[128,2048]{1,0:T(8,128)(2,1)S(1)} %get-tuple-element.249, f32[2048]{0:T(1024)S(1)} %convert_element_type.131, f32[512]{0:T(512)S(1)} %dynamic_slice.34, f32[2048,128]{1,0:T(8,128)S(1)} %get-tuple-element.235, pred[]{:T(512)S(6)} %compare.18, ...), kind=kOutput, calls=%fused_computation.4.clone.1 | convolution fusion | flops 543686656 | bytes 2895360 | tf_op jit(solution)/shard_map/while/body/eval_jaxpr/dot_general | solution.py:105
  174.8 62.8 %psum.70 = f32[128]{0:T(128)S(1)} all-reduce(f32[128]{0:T(128)S(1)} %convolution_bitcast_fusion.5), channel_id=1, replica_groups=mesh['blk'=32,'col'=16] {'blk'}, use_global_device_ids=true, to_apply=%region_5.6 | all-reduce | flops 128 | bytes 1024 | tf_op jit(solution)/shard_map/psum | solution.py:112
  237.7 14.0 %all-gather = f32[16,1,128]{2,1,0:T(1,128)S(1)} all-gather(f32[1,1,128]{2,1,0:T(1,128)S(1)} %fusion.50), channel_id=1, replica_groups=mesh['blk'=32,'col'=16] {'col'}, dimensions={0}, use_global_device_ids=true | all-gather | bytes 8704 | tf_op jit(solution)/shard_map/all_gather | solution.py:120
  251.7 74.9 %all-reduce.4.cloned.1.call-done = f32[2048,128]{1,0:T(8,128)} async-done(((f32[2048,128]{1,0:T(8,128)}), f32[2048,128]{1,0:T(8,128)}) %all-reduce.4.cloned.1.call-update) | async-done | bytes 1048592 | tf_op jit(solution)/shard_map/psum | solution.py:112
  329.2 24.8 %all-reduce.1 = (f32[]{:T(128)}, f32[]{:T(128)}) all-reduce(f32[]{:T(128)} %get-tuple-element.152, f32[]{:T(128)} %get-tuple-element.151), channel_id=1, replica_groups=mesh['blk'=32,'col'=16] {'col'}, use_global_device_ids=true, to_apply=%region_7.8 | all-reduce | flops 2 | bytes 16 | tf_op jit(solution)/shard_map/psum | solution.py:37
  355.9 24.5 %psum.74 = f32[]{:T(128)} all-reduce(f32[]{:T(128)} %get-tuple-element.173), channel_id=1, replica_groups=mesh['blk'=32,'col'=16] {'col'}, use_global_device_ids=true, to_apply=%region_14.15 | all-reduce | flops 1 | bytes 8 | tf_op jit(solution)/shard_map/psum | solution.py:37
  381.8 14.4 %all-gather.2 = f32[16,1,128]{2,1,0:T(1,128)S(1)} all-gather(f32[1,1,128]{2,1,0:T(1,128)S(1)} %bitcast.116), channel_id=1, replica_groups=mesh['blk'=32,'col'=16] {'col'}, dimensions={0}, use_global_device_ids=true | all-gather | bytes 8704 | tf_op jit(solution)/shard_map/all_gather | solution.py:120
  397.4 27.3 %psum.75 = f32[]{:T(128)} all-reduce(f32[]{:T(128)} %get-tuple-element.176), channel_id=1, replica_groups=mesh['blk'=32,'col'=16] {'col'}, use_global_device_ids=true, to_apply=%region_16.17 | all-reduce | flops 1 | bytes 8 | tf_op jit(solution)/shard_map/psum | solution.py:122
  426.7 24.2 %psum.76 = f32[]{:T(128)} all-reduce(f32[]{:T(128)} %multiply_reduce_fusion), channel_id=1, replica_groups=mesh['blk'=32,'col'=16] {'col'}, use_global_device_ids=true, to_apply=%region_18.19 | all-reduce | flops 1 | bytes 8 | tf_op jit(solution)/shard_map/psum | solution.py:37
  452.2 14.1 %all-gather.3 = f32[16,1,128]{2,1,0:T(1,128)S(1)} all-gather(f32[1,1,128]{2,1,0:T(1,128)S(1)} %bitcast.117), channel_id=1, replica_groups=mesh['blk'=32,'col'=16] {'col'}, dimensions={0}, use_global_device_ids=true | all-gather | bytes 8704 | tf_op jit(solution)/shard_map/all_gather | solution.py:120
  467.5 26.1 %psum.77 = f32[]{:T(128)} all-reduce(f32[]{:T(128)} %fusion.21), channel_id=1, replica_groups=mesh['blk'=32,'col'=16] {'col'}, use_global_device_ids=true, to_apply=%region_20.21 | all-reduce | flops 1 | bytes 8 | tf_op jit(solution)/shard_map/psum | solution.py:122
  496.0 45.7 %all-reduce = (f32[2048]{0:T(1024)S(1)}, f32[2048]{0:T(1024)S(1)}) all-reduce(f32[2048]{0:T(1024)S(1)} %bitcast.112, f32[2048]{0:T(1024)S(1)} %bitcast.111), channel_id=1, replica_groups=mesh['blk'=32,'col'=16] {'col'}, use_global_device_ids=true, to_apply=%region_21.22 | all-reduce | flops 4096 | bytes 32768 | tf_op jit(solution)/shard_map/psum | solution.py:132
  (131 shorter events, 48.9 us)
Async XLA Ops:
  7.2 163.2 %copy-start = (bf16[128,16,128]{2,1,0:T(8,128)(2,1)S(1)}, bf16[128,16,128]{2,1,0:T(8,128)(2,1)}, u32[]{:S(2)}) copy-start(bf16[128,16,128]{2,1,0:T(8,128)(2,1)} %param.19) | copy-start | bytes 1572868
  7.2 18.8 %copy-start.8 = (bf16[1024]{0:T(1024)(128)(2,1)S(1)}, bf16[1024]{0:T(1024)(128)(2,1)}, u32[]{:S(2)}) copy-start(bf16[1024]{0:T(1024)(128)(2,1)} %param.13) | copy-start | bytes 6148
  7.2 64.4 %collective-permute-start = (bf16[128,128]{1,0:T(8,128)(2,1)}, bf16[128,128]{1,0:T(8,128)(2,1)S(1)}, u32[]{:S(2)}, u32[]{:S(2)}) collective-permute-start(bf16[128,128]{1,0:T(8,128)(2,1)} %param.17), channel_id=1, source_target_pairs={{0,1},{1,2},{2,3},{3,4},{4,5},{5,6},{6,7},{7,8},{8,9},{9,10},{10,1... | collective-permute-start | bytes 98312 | tf_op jit(solution)/shard_map/ppermute | solution.py:19
  7.2 64.4 %collective-permute-start.1 = (bf16[128,128]{1,0:T(8,128)(2,1)}, bf16[128,128]{1,0:T(8,128)(2,1)S(1)}, u32[]{:S(2)}, u32[]{:S(2)}) collective-permute-start(bf16[128,128]{1,0:T(8,128)(2,1)} %param.17), channel_id=1, source_target_pairs={{0,15},{1,0},{2,1},{3,2},{4,3},{5,4},{6,5},{7,6},{8,7},{9,8},{10,9... | collective-permute-start | bytes 98312 | tf_op jit(solution)/shard_map/ppermute | solution.py:22
  30.5 31.1 %all-to-all-start = ((bf16[32,3,64]{2,1,0:T(4,128)(2,1)}), bf16[32,3,64]{2,1,0:T(4,128)(2,1)S(1)}, u32[]{:S(2)}, u32[]{:S(2)}) async-start(bf16[32,3,64]{2,1,0:T(4,128)(2,1)} %bitcast.8), calls=%async_computation | async-start | bytes 65536 | tf_op jit(solution)/shard_map/all_to_all | solution.py:80
  61.6 41.9 %all-to-all-start.1 = ((bf16[32,64,128]{2,1,0:T(8,128)(2,1)}), bf16[32,64,128]{2,1,0:T(8,128)(2,1)S(1)}, u32[]{:S(2)}, u32[]{:S(2)}) async-start(bf16[32,64,128]{2,1,0:T(8,128)(2,1)} %bitcast.10), calls=%async_computation.1 | async-start | bytes 1048576 | tf_op jit(solution)/shard_map/all_to_all | solution.py:79
  71.4 255.2 %all-reduce.4.cloned.1.call-start = ((), (), s32[]{:S(2)}) async-start(), calls=%async_computation.2 | async-start | bytes 2097152 | tf_op jit(solution)/shard_map/psum | solution.py:112
  71.6 4.6 collective-permute-start.2
  71.6 4.5 collective-permute-start.3
  76.2 4.6 collective-permute-start.4
  76.2 4.8 collective-permute-start.5
  80.7 4.6 collective-permute-start.6
  81.0 4.8 collective-permute-start.7
  85.3 4.6 collective-permute-start.8
  85.9 4.6 collective-permute-start.9
  89.8 4.6 collective-permute-start.10
  90.4 4.6 collective-permute-start.11
  94.4 4.6 collective-permute-start.12
  95.0 4.6 collective-permute-start.13
  98.9 4.6 collective-permute-start.14
  326.6 69.6 %copy-start.1 = (f32[2048,128]{1,0:T(8,128)S(1)}, f32[2048,128]{1,0:T(8,128)}, u32[]{:S(2)}) copy-start(f32[2048,128]{1,0:T(8,128)} %all-reduce.4.cloned.1.call-done) | copy-start | bytes 3145732
  467.5 75.4 %copy-start.9 = (f32[128]{0:T(128)S(1)}, f32[128]{0:T(128)}, u32[]{:S(2)}) copy-start(f32[128]{0:T(128)} %param.20) | copy-start | bytes 1540
  467.5 75.5 %copy-start.11 = (s32[128]{0:T(128)S(1)}, s32[128]{0:T(128)}, u32[]{:S(2)}) copy-start(s32[128]{0:T(128)} %param.21) | copy-start | bytes 1540
  494.9 48.6 %copy-start.5 = (f32[128]{0:T(128)}, f32[128]{0:T(128)S(1)}, u32[]{:S(2)}) copy-start(f32[128]{0:T(128)S(1)} %multiply_add_fusion.1) | copy-start | bytes 1540
  (6 other events, 87.8 us)
Sparse Core Ops, SparseCore 0:
  170.5 156.1 all-reduce.3
